TPU v7x, 256 devices: a whole 4x4x8 slice. The times are simulated.
256 devices in a mesh: expert: 16 (over x_lo, y, core), hidden: 16 (over z, x_hi).
Axes of the slice: x: 4 (x_hi: 2, x_lo: 2; x = x_hi * 2 + x_lo), y: 4, z: 8, core: 2. Of those that a mesh axis runs over, the one named last changes fastest.
Arguments:
- tokens: bfloat16 [4096, 7168], P('expert', 'hidden'), may hold values from -6 to 6
- route_ids: int32 [4096, 2], P('expert'), may hold values from 0 to 15, all different within a row; in each aligned block of 256 rows (0 to 255, 256 to 511, ...) at most 40 rows name the same one
- route_weight: float32 [4096, 2], P('expert'), may hold values from 0.2 to 2
- w_gate: bfloat16 [16, 7168, 2048], P('expert', None, 'hidden'), may hold values from -0.0625 to 0.0625
- w_up: bfloat16 [16, 7168, 2048], P('expert', None, 'hidden'), may hold values from -0.0625 to 0.0625
- w_down: bfloat16 [16, 2048, 7168], P('expert', 'hidden'), may hold values from -0.125 to 0.125
Outputs:
- mixed: bfloat16 [4096, 7168], P('expert', 'hidden')
Inputs may be any that keep to these rules, and one draw needn't show every extreme that they name: `route_ids`: each row names 2 different experts. In the aligned blocks of 256 rows, no expert is named by more than 40 rows of one block, a bound that some block reaches.
All inputs are finite; a program needn't handle non-finite values.
Results may differ from a plain program's by a relative error of at most 0.0057.
Values may be sent and summed in bfloat16 or wider, within the bound.
No kernel may reach another device: no remote copies, remote signals or barrier semaphores. Data moves between devices by JAX's collectives and lax.ppermute only.
A program may use at most 128 MiB of HBM per device.

v0:
```python
import jax
import jax.numpy as jnp
from jax import lax
from jax.sharding import PartitionSpec as P

TOP = 2


def on_device(tokens, route_ids, route_weight, w_gate, w_up, w_down):
    experts = lax.axis_size("expert")
    rows_dev = tokens.shape[0]
    capacity = (rows_dev * TOP * 5 + 4 * experts - 1) // (4 * experts)
    slot_count = experts * capacity
    matches = route_ids[:, :, None] == jnp.arange(experts, dtype=jnp.int32)[None, None, :]
    chosen = jnp.sum(matches.astype(jnp.int32), axis=1)
    ranking = jnp.cumsum(chosen, axis=0) - chosen
    slot_ids = jnp.arange(capacity, dtype=jnp.int32)
    placed = (chosen.T[:, None, :] == 1) & (ranking.T[:, None, :] == slot_ids[None, :, None])
    every_row = lax.all_gather(tokens, "expert", axis=0, tiled=True)
    every_route = lax.all_gather(route_ids, "expert", axis=0, tiled=True)
    own_expert = lax.axis_index("expert")
    flagged = jnp.sum((every_route == own_expert).astype(jnp.int32), axis=1).reshape(
        experts, rows_dev
    )
    ordering = jnp.cumsum(flagged, axis=1) - flagged
    picks = (flagged[:, None, :] == 1) & (ordering[:, None, :] == slot_ids[None, :, None])
    arrived = jnp.einsum(
        "sct,std->scd",
        picks.astype(jnp.bfloat16),
        every_row.reshape(experts, rows_dev, -1),
        preferred_element_type=jnp.float32,
    ).astype(jnp.bfloat16)
    flat_rows = arrived.reshape(slot_count, -1)
    gate_w = w_gate[0]
    up_w = w_up[0]
    down_w = w_down[0]
    fragment = lax.all_gather(flat_rows, "hidden", axis=1, tiled=True)
    gate_sum = jnp.dot(fragment, gate_w, preferred_element_type=jnp.float32)
    up_sum = jnp.dot(fragment, up_w, preferred_element_type=jnp.float32)
    hidden = (jax.nn.silu(gate_sum) * up_sum).astype(jnp.bfloat16)
    partials = jnp.dot(hidden, down_w, preferred_element_type=jnp.float32)
    produced = lax.psum_scatter(partials, "hidden", scatter_dimension=1, tiled=True)
    produced = produced.astype(jnp.bfloat16).reshape(experts, capacity, -1)
    returned = lax.all_to_all(produced, "expert", split_axis=0, concat_axis=0, tiled=True)
    per_expert = jnp.sum(jnp.where(matches, route_weight[:, :, None], jnp.float32(0.0)), axis=1)
    combine_table = placed.astype(jnp.float32) * per_expert.T[:, None, :]
    mixed = jnp.einsum(
        "ect,ecd->td", combine_table, returned.astype(jnp.float32), precision=lax.Precision.HIGHEST
    )
    return mixed.astype(jnp.bfloat16)


def solution(mesh):
    in_specs = (
        P("expert", "hidden"),
        P("expert", None),
        P("expert", None),
        P("expert", None, "hidden"),
        P("expert", None, "hidden"),
        P("expert", "hidden", None),
    )
    out_specs = P("expert", "hidden")
    return jax.shard_map(
        on_device, mesh=mesh, in_specs=in_specs, out_specs=out_specs, check_vma=False
    )
```

profile of v0, /device:TPU:1, one launch (start us, length us, event | category | flops | bytes accessed | tf_op | source)
XLA Modules:
  0.0 564.6 jit_solution(8759587761792712818)
XLA Ops:
  6.5 0.7 all-gather.3.cloned.1.call-update
  7.3 0.0 all-gather.5.cloned.1.call-start
  7.3 21.5 %all_gather.9 = s32[4096,2]{0,1:T(2,128)S(1)} all-gather(s32[256,2]{0,1:T(2,128)} %param.7), channel_id=1, replica_groups=mesh['expert'=16,'hidden'=16] {'expert'}, dimensions={0}, use_global_device_ids=true | all-gather | bytes 34816 | tf_op jit(solution)/shard_map/all_gather | solution.py:20
  28.9 0.6 reduce-window.16
  29.5 0.2 slice_reduce_fusion
  29.7 0.1 bitcast_subtract_fusion
  29.8 30.3 %all-gather.3.cloned.1.call-done = bf16[4096,448]{0,1:T(8,128)(2,1)} async-done(((bf16[256,448]{0,1:T(8,128)(2,1)}), bf16[4096,448]{0,1:T(8,128)(2,1)}) %all-gather.3.cloned.1.call-update) | async-done | bytes 3670032 | tf_op jit(solution)/shard_map/all_gather | solution.py:19
  60.1 3.2 fusion.9
  63.3 1.1 copy.32
  64.4 0.0 all-gather.5.cloned.1.call-update
  64.4 0.0 reduce-scatter.2.cloned.1.call-start
  64.4 142.2 %all-gather.5.cloned.1.call-done = bf16[640,7168]{0,1:T(8,128)(2,1)} async-done(((bf16[640,448]{0,1:T(8,128)(2,1)}), bf16[640,7168]{0,1:T(8,128)(2,1)}) %all-gather.5.cloned.1.call-update) | async-done | bytes 9175056 | tf_op jit(solution)/shard_map/all_gather | solution.py:37
  206.6 6.7 %fusion.7 = f32[640,128]{1,0:T(8,128)S(1)} fusion(bf16[640,7168]{0,1:T(8,128)(2,1)} %all-gather.5.cloned.1.call-done, bf16[1,7168,128]{2,1,0:T(8,128)(2,1)} %param.9), kind=kOutput, calls=%fused_computation.7 | convolution fusion | flops 1174405120 | bytes 11337728 | tf_op jit(solution)/shard_map/dot_general | solution.py:38
  213.3 20.0 %fusion.3 = f32[640,7168]{0,1:T(8,128)} fusion(bf16[1,128,7168]{2,1,0:T(8,128)(2,1)S(1)} %copy-done, bf16[640,7168]{0,1:T(8,128)(2,1)} %all-gather.5.cloned.1.call-done, bf16[1,7168,128]{2,1,0:T(8,128)(2,1)} %param.10, f32[640,128]{1,0:T(8,128)S(1)} %fusion.7), kind=kOutput, calls=%fused_computation.3 | convolution fusion | flops 2349301760 | bytes 31522816 | tf_op jit(solution)/shard_map/dot_general | solution.py:41
  233.4 0.7 copy-done.1
  234.1 0.6 reduce-window.14
  234.6 0.2 slice_reduce_fusion.1
  234.9 302.3 %reduce-scatter.2.cloned.1.call-done = f32[640,448]{0,1:T(8,128)} async-done(((f32[640,7168]{0,1:T(8,128)}), f32[640,448]{0,1:T(8,128)}) %reduce-scatter.2.cloned.1.call-update) | async-done | bytes 1146896 | tf_op jit(solution)/shard_map/reduce_scatter | solution.py:42
  537.1 1.3 convert_element_type.25
  538.5 1.1 copy.33
  539.6 5.5 all-to-all-start
  545.1 0.1 bitcast_subtract_fusion.1
  545.2 11.1 %all-to-all-done = bf16[16,40,448]{2,1,0:T(8,128)(2,1)S(1)} async-done(((bf16[16,40,448]{2,1,0:T(8,128)(2,1)}), bf16[16,40,448]{2,1,0:T(8,128)(2,1)S(1)}, u32[]{:S(2)}, u32[]{:S(2)}) %all-to-all-start) | async-done | bytes 573472 | tf_op jit(solution)/shard_map/all_to_all | solution.py:44
  556.4 1.7 fusion.12
  (19 shorter events, 0.2 us)
Async XLA Ops:
  6.5 206.8 %copy-start = (bf16[1,128,7168]{2,1,0:T(8,128)(2,1)S(1)}, bf16[1,128,7168]{2,1,0:T(8,128)(2,1)}, u32[]{:S(2)}) copy-start(bf16[1,128,7168]{2,1,0:T(8,128)(2,1)} %param.11) | copy-start | bytes 5505028
  6.5 53.6 %all-gather.3.cloned.1.call-start = ((), (), s32[]{:S(2)}) async-start(), calls=%async_computation.2 | async-start | bytes 3899392 | tf_op jit(solution)/shard_map/all_gather | solution.py:19
  7.3 199.4 %all-gather.5.cloned.1.call-start = ((), (), s32[]{:S(2)}) async-start(), calls=%async_computation.3 | async-start | bytes 9748480 | tf_op jit(solution)/shard_map/all_gather | solution.py:37
  64.4 472.8 %reduce-scatter.2.cloned.1.call-start = ((), (), s32[]{:S(2)}) async-start(), calls=%async_computation.4 | async-start | bytes 19496960 | tf_op jit(solution)/shard_map/reduce_scatter | solution.py:42
  233.4 0.7 copy-start.1
  234.0 311.1 %copy-start.2 = (f32[256,2]{0,1:T(2,128)S(1)}, f32[256,2]{0,1:T(2,128)}, u32[]{:S(2)}) copy-start(f32[256,2]{0,1:T(2,128)} %param.8) | copy-start | bytes 6148
  539.6 16.8 %all-to-all-start = ((bf16[16,40,448]{2,1,0:T(8,128)(2,1)}), bf16[16,40,448]{2,1,0:T(8,128)(2,1)S(1)}, u32[]{:S(2)}, u32[]{:S(2)}) async-start(bf16[16,40,448]{2,1,0:T(8,128)(2,1)} %bitcast.7), calls=%async_computation.1 | async-start | bytes 1310720 | tf_op jit(solution)/shard_map/all_to_all | solution.py:44
Sparse Core Ops, SparseCore 0:
  9.1 50.9 all-gather.2
  64.5 142.0 all-gather.4
  233.5 303.5 reduce-scatter.1
where the time goes:
time: 565 us
  waiting for transfers between devices  487 us (86%)
  matrix products  31.6 us (6%)
  blocking collectives  21.5 us (4%)
  between operations  13.2 us (2%)
    reduce_scatter x1, waiting for transfers between devices, on_device(): lax.psum_scatter(partials, 'hidden', scatter_dimension=1, tiled=True)  302 us
    all_gather x1, waiting for transfers between devices, on_device(): fragment = lax.all_gather(flat_rows, 'hidden', axis=1, tiled=True)  142 us
    all_gather x1, waiting for transfers between devices, on_device(): every_row = lax.all_gather(tokens, 'expert', axis=0, tiled=True)  30.3 us
    all_gather x1, blocking collectives, on_device(): every_route = lax.all_gather(route_ids, 'expert', axis=0, tiled=True)  21.5 us
    dot_general x1, matrix products, on_device(): partials = jnp.dot(hidden, down_w, preferred_element_type=jnp.float32)  20 us
  transfers between devices with their start and end apart: 4, of which 4 were waited for; matrix products, arithmetic and copies ran while one was open for 0% of the time, Pallas kernels for 0%

commit v1 on v0

--- a/solution.py
+++ b/solution.py
@@ -16,7 +16,10 @@
     ranking = jnp.cumsum(chosen, axis=0) - chosen
     slot_ids = jnp.arange(capacity, dtype=jnp.int32)
     placed = (chosen.T[:, None, :] == 1) & (ranking.T[:, None, :] == slot_ids[None, :, None])
-    every_row = lax.all_gather(tokens, "expert", axis=0, tiled=True)
+    every_row = jnp.concatenate(
+        lax.all_to_all(jnp.stack([tokens] * lax.axis_size("expert"), axis=0), "expert", 0, 0),
+        axis=0,
+    )
     every_route = lax.all_gather(route_ids, "expert", axis=0, tiled=True)
     own_expert = lax.axis_index("expert")
     flagged = jnp.sum((every_route == own_expert).astype(jnp.int32), axis=1).reshape(

time: 565 us -> 587 us (1.039)
  blocking collectives: 21.5 us -> 62.3 us
  waiting for transfers between devices: 487 us -> 457 us
  starting transfers between devices: 5.63 us -> 13.2 us
    all_gather x1, blocking collectives: 21.5 us -> 62.3 us  [on_device(): every_route = lax.all_gather(route_ids, 'expert', axis=0, tiled=True)]
    all_gather x1 -> x0, waiting for transfers between devices: 30.3 us -> none  [on_device(): every_row = lax.all_gather(tokens, 'expert', axis=0, tiled=True)]
    all_to_all x0 -> x1, starting transfers between devices: none -> 7.6 us  [on_device(): lax.all_to_all(jnp.stack([tokens] * lax.axis_size('expert'), axis=0), 'ex...]
  transfers between devices with their start and end apart: 4 -> 4, of which waited for: 4 -> 3; matrix products, arithmetic and copies ran while one was open for 0% -> 0% of each run, Pallas kernels for 0% -> 0%
where the time goes in v1:
time: 587 us; the launch traced here: 586 us
  waiting for transfers between devices  457 us (78%)
  blocking collectives  62.3 us (11%)
  matrix products  31.6 us (5%)
  between operations  13.5 us (2%)
  starting transfers between devices  13.2 us (2%)
    reduce_scatter x1, waiting for transfers between devices, on_device(): lax.psum_scatter(partials, 'hidden', scatter_dimension=1, tiled=True)  303 us
    all_gather x1, waiting for transfers between devices, on_device(): fragment = lax.all_gather(flat_rows, 'hidden', axis=1, tiled=True)  143 us
    all_gather x1, blocking collectives, on_device(): every_route = lax.all_gather(route_ids, 'expert', axis=0, tiled=True)  62.3 us
    dot_general x1, matrix products, on_device(): partials = jnp.dot(hidden, down_w, preferred_element_type=jnp.float32)  20 us
  transfers between devices with their start and end apart: 4, of which 3 were waited for; matrix products, arithmetic and copies ran while one was open for 0% of the time, Pallas kernels for 0%

profile of v1, /device:TPU:1, one launch (start us, length us, event | category | flops | bytes accessed | tf_op | source)
XLA Modules:
  0.0 586.2 jit_solution(5995481655962362099)
XLA Ops:
  6.5 3.3 stack.2
  9.8 7.6 %all-to-all-start = ((bf16[16,256,448]{1,2,0:T(8,128)(2,1)}), bf16[16,256,448]{1,2,0:T(8,128)(2,1)}, u32[]{:S(2)}, u32[]{:S(2)}) async-start(bf16[16,256,448]{1,2,0:T(8,128)(2,1)} %stack.2), calls=%async_computation | async-start | bytes 7340032 | tf_op jit(solution)/shard_map/all_to_all | solution.py:20
  17.4 0.0 all-gather.2.cloned.1.call-start
  17.5 62.3 %all_gather.6 = s32[4096,2]{0,1:T(2,128)S(1)} all-gather(s32[256,2]{0,1:T(2,128)S(1)} %copy-done.1), channel_id=1, replica_groups=mesh['expert'=16,'hidden'=16] {'expert'}, dimensions={0}, use_global_device_ids=true | all-gather | bytes 34816 | tf_op jit(solution)/shard_map/all_gather | solution.py:23
  79.8 0.6 reduce-window.16
  80.4 0.2 slice_reduce_fusion
  80.6 0.1 bitcast_subtract_fusion
  80.7 3.2 convolution_convert_fusion
  83.9 1.1 copy.29
  84.9 0.0 all-gather.2.cloned.1.call-update
  85.0 0.0 reduce-scatter.2.cloned.1.call-start
  85.0 143.0 %all-gather.2.cloned.1.call-done = bf16[640,7168]{0,1:T(8,128)(2,1)} async-done(((bf16[640,448]{0,1:T(8,128)(2,1)}), bf16[640,7168]{0,1:T(8,128)(2,1)}) %all-gather.2.cloned.1.call-update) | async-done | bytes 9175056 | tf_op jit(solution)/shard_map/all_gather | solution.py:40
  228.1 6.7 %fusion.4 = f32[640,128]{1,0:T(8,128)S(1)} fusion(bf16[640,7168]{0,1:T(8,128)(2,1)} %all-gather.2.cloned.1.call-done, bf16[1,7168,128]{2,1,0:T(8,128)(2,1)} %param.9), kind=kOutput, calls=%fused_computation.4 | convolution fusion | flops 1174405120 | bytes 11337728 | tf_op jit(solution)/shard_map/dot_general | solution.py:41
  234.8 20.0 %fusion = f32[640,7168]{0,1:T(8,128)} fusion(bf16[1,128,7168]{2,1,0:T(8,128)(2,1)S(1)} %copy-done, bf16[640,7168]{0,1:T(8,128)(2,1)} %all-gather.2.cloned.1.call-done, bf16[1,7168,128]{2,1,0:T(8,128)(2,1)} %param.10, f32[640,128]{1,0:T(8,128)S(1)} %fusion.4), kind=kOutput, calls=%fused_computation | convolution fusion | flops 2349301760 | bytes 31522816 | tf_op jit(solution)/shard_map/dot_general | solution.py:44
  254.8 0.0 reduce-scatter.2.cloned.1.call-update
  254.9 0.6 reduce-window.14
  255.4 0.2 slice_reduce_fusion.1
  255.7 302.8 %reduce-scatter.2.cloned.1.call-done = f32[640,448]{0,1:T(8,128)} async-done(((f32[640,7168]{0,1:T(8,128)}), f32[640,448]{0,1:T(8,128)}) %reduce-scatter.2.cloned.1.call-update) | async-done | bytes 1146896 | tf_op jit(solution)/shard_map/reduce_scatter | solution.py:45
  558.4 1.3 convert_element_type.25
  559.8 1.1 copy.30
  560.9 5.5 all-to-all-start.1
  566.4 0.1 bitcast_subtract_fusion.1
  566.5 11.1 %all-to-all-done.1 = bf16[16,40,448]{2,1,0:T(8,128)(2,1)S(1)} async-done(((bf16[16,40,448]{2,1,0:T(8,128)(2,1)}), bf16[16,40,448]{2,1,0:T(8,128)(2,1)S(1)}, u32[]{:S(2)}, u32[]{:S(2)}) %all-to-all-start.1) | async-done | bytes 573472 | tf_op jit(solution)/shard_map/all_to_all | solution.py:47
  577.7 1.7 fusion.6
  (19 shorter events, 0.2 us)
Async XLA Ops:
  6.5 228.2 %copy-start = (bf16[1,128,7168]{2,1,0:T(8,128)(2,1)S(1)}, bf16[1,128,7168]{2,1,0:T(8,128)(2,1)}, u32[]{:S(2)}) copy-start(bf16[1,128,7168]{2,1,0:T(8,128)(2,1)} %param.11) | copy-start | bytes 5505028
  9.8 7.7 %copy-start.1 = (s32[256,2]{0,1:T(2,128)S(1)}, s32[256,2]{0,1:T(2,128)}, u32[]{:S(2)}) copy-start(s32[256,2]{0,1:T(2,128)} %param.7) | copy-start | bytes 6148
  9.8 70.9 %all-to-all-start = ((bf16[16,256,448]{1,2,0:T(8,128)(2,1)}), bf16[16,256,448]{1,2,0:T(8,128)(2,1)}, u32[]{:S(2)}, u32[]{:S(2)}) async-start(bf16[16,256,448]{1,2,0:T(8,128)(2,1)} %stack.2), calls=%async_computation | async-start | bytes 7340032 | tf_op jit(solution)/shard_map/all_to_all | solution.py:20
  17.4 210.7 %all-gather.2.cloned.1.call-start = ((), (), s32[]{:S(2)}) async-start(), calls=%async_computation.3 | async-start | bytes 9748480 | tf_op jit(solution)/shard_map/all_gather | solution.py:40
  85.0 473.5 %reduce-scatter.2.cloned.1.call-start = ((), (), s32[]{:S(2)}) async-start(), calls=%async_computation.4 | async-start | bytes 19496960 | tf_op jit(solution)/shard_map/reduce_scatter | solution.py:45
  254.8 311.6 %copy-start.2 = (f32[256,2]{0,1:T(2,128)S(1)}, f32[256,2]{0,1:T(2,128)}, u32[]{:S(2)}) copy-start(f32[256,2]{0,1:T(2,128)} %param.8) | copy-start | bytes 6148
  560.9 16.8 %all-to-all-start.1 = ((bf16[16,40,448]{2,1,0:T(8,128)(2,1)}), bf16[16,40,448]{2,1,0:T(8,128)(2,1)S(1)}, u32[]{:S(2)}, u32[]{:S(2)}) async-start(bf16[16,40,448]{2,1,0:T(8,128)(2,1)} %bitcast.7), calls=%async_computation.2 | async-start | bytes 1310720 | tf_op jit(solution)/shard_map/all_to_all | solution.py:47
Sparse Core Ops, SparseCore 0:
  85.1 142.9 all-gather.1
  254.9 303.4 reduce-scatter.1
